TPU v7x, 128 devices: a whole 4x4x4 slice. The times are simulated.
128 devices in a mesh: dp: 8 (over x, z_hi), vocab: 16 (over z_lo, y, core).
Axes of the slice: x: 4, y: 4, z: 4 (z_hi: 2, z_lo: 2; z = z_hi * 2 + z_lo), core: 2. Of those that a mesh axis runs over, the one named last changes fastest.
Arguments:
- query_hidden: bfloat16 [16, 128, 4096], P('dp', None, 'vocab'), may hold values from -144 to 144
- passage_hidden: bfloat16 [16, 256, 4096], P('dp', None, 'vocab'), may hold values from -144 to 144
- head_weight: bfloat16 [4096, 32768], P(None, 'vocab'), may hold values from -6 to 6
- query_mask: int32 [16, 128], P('dp'), may hold values from 0 to 1, as said below
- passage_mask: int32 [16, 256], P('dp'), may hold values from 0 to 1, as said below
- positive: int32 [16], replicated, may hold values from 0 to 15
Outputs:
- grad_query_hidden: bfloat16 [16, 128, 4096], P('dp', None, 'vocab')
- grad_passage_hidden: bfloat16 [16, 256, 4096], P('dp', None, 'vocab')
- query_loss: float32 [16], P('dp')
Inputs may be any that keep to these rules, and one draw needn't show every extreme that they name: `query_mask`: the live tokens of each query are a prefix of 32 to 128 positions. `passage_mask`: the live tokens of each passage are a prefix of 64 to 256 positions.
All inputs are finite; a program needn't handle non-finite values.
Results may differ from a plain program's by a relative error of at most 0.0095.
Values may be sent and summed in bfloat16 or wider, within the bound.
No kernel may reach another device: no remote copies, remote signals or barrier semaphores. Data moves between devices by JAX's collectives and lax.ppermute only.
A program may use at most 128 MiB of HBM per device.

v0:
```python
import jax
import jax.numpy as jnp
from jax import lax
from jax.sharding import PartitionSpec as P

normalizer_sharpness = 0.2
score_div = 16.0
loss_scale = 65536.0


def pooling_row_block(lexicon_projection_lines, live):
    divided_similarity_matrix = lexicon_projection_lines / normalizer_sharpness
    live_rows = live[:, :, None] > 0
    largest_element = jnp.max(jnp.where(live_rows, divided_similarity_matrix, -1e30), axis=1)
    expo = jnp.where(
        live_rows, jnp.exp(divided_similarity_matrix - largest_element[:, None, :]), 0.0
    )
    cumulative_accumulator = jnp.sum(expo, axis=1)
    softened_rectifier_output = normalizer_sharpness * (
        largest_element + jnp.log(cumulative_accumulator)
    )
    return (softened_rectifier_output, expo / cumulative_accumulator[:, None, :])


def exact_dot(left, right):
    return jnp.dot(left, right, precision=lax.Precision.HIGHEST, preferred_element_type=jnp.float32)


def loss_and_grad(scores, targets, total_queries):
    largest_element = jnp.max(scores, axis=1)
    lse = largest_element + jnp.log(jnp.sum(jnp.exp(scores - largest_element[:, None]), axis=1))
    picked = (targets[:, None] == jnp.arange(scores.shape[1], dtype=jnp.int32)[None, :]).astype(
        jnp.float32
    )
    losses = lse - jnp.sum(scores * picked, axis=1)
    probs = jnp.exp(scores - lse[:, None])
    return (losses, (probs - picked) * (loss_scale / total_queries))


def token_grads(dpooled, softened_rectifier_output, share):
    dsmooth = dpooled * jnp.where(
        softened_rectifier_output > 0,
        1.0 / (1.0 + jnp.maximum(softened_rectifier_output, 0.0)),
        0.0,
    )
    dlogits = (share * dsmooth[:, None, :]).astype(jnp.bfloat16)
    return dlogits.reshape(dlogits.shape[0] * dlogits.shape[1], dlogits.shape[2])


def on_device(query_hidden, passage_hidden, head_weight, query_mask, passage_mask, positive):
    q_count, q_len, width_part = query_hidden.shape
    p_count, p_len, _ = passage_hidden.shape
    columns = head_weight.shape[1]
    split = q_count * q_len
    tokens = jnp.concatenate(
        [
            query_hidden.reshape(split, width_part),
            passage_hidden.reshape(p_count * p_len, width_part),
        ],
        axis=0,
    )
    w_rows = head_weight
    lexicon_projection_lines = jnp.dot(
        lax.all_gather(tokens, "vocab", axis=1, tiled=True),
        w_rows,
        preferred_element_type=jnp.float32,
    )
    q_smooth, q_share = pooling_row_block(
        lexicon_projection_lines[:split].reshape(q_count, q_len, columns), query_mask
    )
    p_smooth, p_share = pooling_row_block(
        lexicon_projection_lines[split:].reshape(p_count, p_len, columns), passage_mask
    )
    q_pooled = jnp.log1p(jnp.maximum(q_smooth, 0.0))
    p_pooled = jnp.log1p(jnp.maximum(p_smooth, 0.0))
    group = lax.axis_index("dp")
    total_queries = positive.shape[0]
    p_every = lax.all_gather(p_pooled, "dp", axis=0, tiled=True)
    scores = lax.psum(exact_dot(q_pooled, p_every.T), "vocab") / score_div
    targets = lax.dynamic_slice_in_dim(positive, group * q_count, q_count, 0)
    query_loss, dscores = loss_and_grad(scores, targets, total_queries)
    dq_pooled = exact_dot(dscores, p_every) / score_div
    grad_passage_summary = lax.psum_scatter(
        exact_dot(dscores.T, q_pooled) / score_div, "dp", scatter_dimension=0, tiled=True
    )
    dlogits = jnp.concatenate(
        [
            token_grads(dq_pooled, q_smooth, q_share),
            token_grads(grad_passage_summary, p_smooth, p_share),
        ],
        axis=0,
    )
    w_rows = head_weight
    own_grad = lax.psum_scatter(
        lax.dot_general(
            w_rows, dlogits, (((1,), (1,)), ((), ())), preferred_element_type=jnp.float32
        ),
        "vocab",
        scatter_dimension=0,
        tiled=True,
    ).T
    own_grad = own_grad.astype(jnp.bfloat16)
    grad_query_hidden = own_grad[:split].reshape(q_count, q_len, width_part)
    grad_passage_hidden = own_grad[split:].reshape(p_count, p_len, width_part)
    return (grad_query_hidden, grad_passage_hidden, query_loss)


def solution(mesh):
    return jax.shard_map(
        on_device,
        mesh=mesh,
        in_specs=(
            P("dp", None, "vocab"),
            P("dp", None, "vocab"),
            P(None, "vocab"),
            P("dp", None),
            P("dp", None),
            P(),
        ),
        out_specs=(P("dp", None, "vocab"), P("dp", None, "vocab"), P("dp")),
        check_vma=False,
    )
```

profile of v0, /device:TPU:0, one launch (start us, length us, event | category | flops | bytes accessed | tf_op | source)
XLA Modules:
  0.0 344.2 jit_solution(16631525663870407592)
XLA Ops:
  7.2 0.0 all-gather.3.cloned.1.call-start
  7.2 1.8 pad_maximum_fusion
  9.0 0.0 all-gather.3.cloned.1.call-update
  9.0 0.0 all-reduce.3.cloned.1.call-start
  9.1 0.7 broadcast_compare_fusion
  9.8 1.2 dynamic-slice
  11.7 0.7 dynamic_slice.3
  12.4 0.7 broadcast_compare_fusion.1
  13.1 0.7 fusion.29
  13.8 50.4 %all-gather.3.cloned.1.call-done = bf16[768,4096]{1,0:T(8,128)(2,1)} async-done(((bf16[768,256]{1,0:T(8,128)(2,1)}), bf16[768,4096]{1,0:T(8,128)(2,1)}) %all-gather.3.cloned.1.call-update) | async-done | bytes 6291472 | tf_op jit(solution)/shard_map/all_gather | solution.py:64
  64.2 17.7 %fusion.23 = f32[768,2048]{1,0:T(8,128)S(1)} fusion(bf16[768,4096]{1,0:T(8,128)(2,1)} %all-gather.3.cloned.1.call-done, bf16[4096,2048]{1,0:T(8,128)(2,1)} %param.8), kind=kOutput, calls=%fused_computation.53 | convolution fusion | flops 12884901888 | bytes 29360128 | tf_op jit(solution)/shard_map/dot_general | solution.py:63
  81.9 0.0 copy-start
  81.9 0.6 select_reduce_fusion.1
  82.5 0.3 select_reduce_fusion.3
  82.9 0.5 select_reduce_fusion.2
  83.3 1.2 copy-done
  84.6 0.9 select_reduce_fusion
  85.6 34.2 %all-gather = f32[8,2,2048]{2,1,0:T(2,128)S(1)} all-gather(f32[1,2,2048]{2,1,0:T(2,128)S(1)} %log-plus-one_bitcast_fusion), channel_id=1, replica_groups=mesh['dp'=8,'vocab'=16] {'dp'}, dimensions={0}, use_global_device_ids=true | all-gather | bytes 147456 | tf_op jit(solution)/shard_map/all_gather | solution.py:78
  119.8 0.1 reshape.58
  119.9 0.2 fusion.12
  120.1 27.2 %psum.7 = f32[2,16]{1,0:T(2,128)S(1)} all-reduce(f32[2,16]{1,0:T(2,128)S(1)} %fusion.12), channel_id=1, replica_groups=mesh['dp'=8,'vocab'=16] {'vocab'}, use_global_device_ids=true, to_apply=%region_4.5 | all-reduce | flops 32 | bytes 256 | tf_op jit(solution)/shard_map/psum | solution.py:79
  147.3 0.1 fusion.18
  147.4 0.2 select_reduce_fusion.4
  147.7 0.5 fusion.22
  148.2 1.1 convolution_multiply_fusion
  149.3 0.0 all-reduce.3.cloned.1.call-update
  149.3 0.2 reduce-scatter.2.cloned.1.call-start
  149.5 0.3 fusion.6
  149.8 2.2 fusion.7
  152.0 79.7 %all-reduce.3.cloned.1.call-done = f32[16,2048]{1,0:T(8,128)} async-done(((f32[16,2048]{1,0:T(8,128)}), f32[16,2048]{1,0:T(8,128)}) %all-reduce.3.cloned.1.call-update) | async-done | bytes 131088
  231.6 0.9 fusion.10
  232.5 3.0 fusion
  235.5 19.4 %convolution_bitcast_fusion = f32[4096,768]{0,1:T(8,128)} fusion(bf16[4096,2048]{1,0:T(8,128)(2,1)} %param.8, bf16[512,2048]{1,0:T(8,128)(2,1)S(1)} %fusion, bf16[256,2048]{1,0:T(8,128)(2,1)S(1)} %fusion.7), kind=kOutput, calls=%fused_computation | convolution fusion | flops 12891193344 | bytes 32505856 | tf_op jit(solution)/shard_map/dot_general | solution.py:95
  254.9 0.0 reduce-scatter.2.cloned.1.call-update
  254.9 80.2 %reduce-scatter.2.cloned.1.call-done = f32[256,768]{0,1:T(8,128)} async-done(((f32[4096,768]{0,1:T(8,128)}), f32[256,768]{0,1:T(8,128)}) %reduce-scatter.2.cloned.1.call-update) | async-done | bytes 786448 | tf_op jit(solution)/shard_map/reduce_scatter | solution.py:94
  335.1 1.2 convert_bitcast_fusion
  336.3 0.7 slice.18
  337.0 0.7 slice.19
  (2 shorter events, 0.1 us)
Async XLA Ops:
  7.2 57.0 %all-gather.3.cloned.1.call-start = ((), (), s32[]{:S(2)}) async-start(), calls=%async_computation.1 | async-start | bytes 6684672 | tf_op jit(solution)/shard_map/all_gather | solution.py:64
  9.0 222.6 %all-reduce.3.cloned.1.call-start = ((), (), s32[]{:S(2)}) async-start(), calls=%async_computation.3 | async-start | bytes 262144
  81.9 2.7 copy-start
  149.3 185.8 %reduce-scatter.2.cloned.1.call-start = ((), (), s32[]{:S(2)}) async-start(), calls=%async_computation.2 | async-start | bytes 13369344 | tf_op jit(solution)/shard_map/reduce_scatter | solution.py:94
Sparse Core Ops, SparseCore 0:
  9.6 54.5 all-gather.2
  149.4 82.1 all-reduce.2
  255.0 80.0 reduce-scatter.1
where the time goes:
time: 345 us; the launch traced here: 344 us
  waiting for transfers between devices  210 us (61%)
  blocking collectives  61.4 us (18%)
  matrix products  38.7 us (11%)
  between operations  14.5 us (4%)
  other arithmetic  14.3 us (4%)
  local copies, waits for them, and re-layouts  4.7 us (1%)
    reduce_scatter x1, waiting for transfers between devices, on_device(): lax.psum_scatter(lax.dot_general(w_rows, dlogits, (((1,), (1,)), ((), ())...  80.2 us
    unnamed x4, waiting for transfers between devices  79.7 us
    all_gather x1, waiting for transfers between devices, on_device(): lax.all_gather(tokens, 'vocab', axis=1, tiled=True)  50.4 us
    all_gather x1, blocking collectives, on_device(): p_every = lax.all_gather(p_pooled, 'dp', axis=0, tiled=True)  34.2 us
    psum x1, blocking collectives, on_device(): scores = lax.psum(exact_dot(q_pooled, p_every.T), 'vocab') / score_div  27.2 us
    dot_general x1, matrix products, on_device(): lax.dot_general(w_rows, dlogits, (((1,), (1,)), ((), ())), preferred_elem...  19.4 us
    dot_general x1, matrix products, on_device(): jnp.dot(lax.all_gather(tokens, 'vocab', axis=1, tiled=True), w_rows, pref...  17.7 us
  transfers between devices with their start and end apart: 3, of which 3 were waited for; matrix products, arithmetic and copies ran while one was open for 2% of the time, Pallas kernels for 0%

commit v1 on v0

--- a/solution.py
+++ b/solution.py
@@ -75,7 +75,9 @@
     p_pooled = jnp.log1p(jnp.maximum(p_smooth, 0.0))
     group = lax.axis_index("dp")
     total_queries = positive.shape[0]
-    p_every = lax.all_gather(p_pooled, "dp", axis=0, tiled=True)
+    p_every = jnp.concatenate(
+        lax.all_to_all(jnp.stack([p_pooled] * lax.axis_size("dp")), "dp", 0, 0), axis=0
+    )
     scores = lax.psum(exact_dot(q_pooled, p_every.T), "vocab") / score_div
     targets = lax.dynamic_slice_in_dim(positive, group * q_count, q_count, 0)
     query_loss, dscores = loss_and_grad(scores, targets, total_queries)

time: 345 us -> 323 us (0.936)
  blocking collectives: 61.4 us -> 27.2 us
  starting transfers between devices: 0.3 us -> 7.18 us
  waiting for transfers between devices: 210 us -> 214 us
    all_gather x1 -> x0, blocking collectives: 34.2 us -> none  [on_device(): p_every = lax.all_gather(p_pooled, 'dp', axis=0, tiled=True)]
    all_to_all x0 -> x1, starting transfers between devices: none -> 6.88 us  [on_device(): lax.all_to_all(jnp.stack([p_pooled] * lax.axis_size('dp')), 'dp', 0, 0)]
    all_to_all x0 -> x1, waiting for transfers between devices: none -> 5.79 us  [on_device(): lax.all_to_all(jnp.stack([p_pooled] * lax.axis_size('dp')), 'dp', 0, 0)]
  transfers between devices with their start and end apart: 3 -> 4, of which waited for: 3 -> 4; matrix products, arithmetic and copies ran while one was open for 2% -> 3% of each run, Pallas kernels for 0% -> 0%
where the time goes in v1:
time: 323 us; the launch traced here: 322 us
  waiting for transfers between devices  214 us (66%)
  matrix products  38.7 us (12%)
  blocking collectives  27.2 us (8%)
  other arithmetic  15.9 us (5%)
  between operations  14.5 us (4%)
  starting transfers between devices  7.18 us (2%)
  local copies, waits for them, and re-layouts  4.93 us (2%)
    reduce_scatter x1, waiting for transfers between devices, on_device(): lax.psum_scatter(lax.dot_general(w_rows, dlogits, (((1,), (1,)), ((), ())...  80.2 us
    unnamed x4, waiting for transfers between devices  77.5 us
    all_gather x1, waiting for transfers between devices, on_device(): lax.all_gather(tokens, 'vocab', axis=1, tiled=True)  50.4 us
    psum x1, blocking collectives, on_device(): scores = lax.psum(exact_dot(q_pooled, p_every.T), 'vocab') / score_div  27.2 us
    dot_general x1, matrix products, on_device(): lax.dot_general(w_rows, dlogits, (((1,), (1,)), ((), ())), preferred_elem...  19.4 us
    dot_general x1, matrix products, on_device(): jnp.dot(lax.all_gather(tokens, 'vocab', axis=1, tiled=True), w_rows, pref...  17.7 us
    all_to_all x1, starting transfers between devices, on_device(): lax.all_to_all(jnp.stack([p_pooled] * lax.axis_size('dp')), 'dp', 0, 0)  6.88 us
  transfers between devices with their start and end apart: 4, of which 4 were waited for; matrix products, arithmetic and copies ran while one was open for 3% of the time, Pallas kernels for 0%

profile of v1, /device:TPU:0, one launch (start us, length us, event | category | flops | bytes accessed | tf_op | source)
XLA Modules:
  0.0 322.4 jit_solution(14731936501507302420)
XLA Ops:
  7.2 0.0 all-gather.2.cloned.1.call-start
  7.2 1.8 pad_maximum_fusion
  9.0 0.0 all-gather.2.cloned.1.call-update
  9.0 0.7 broadcast_compare_fusion
  9.7 1.2 dynamic-slice
  11.6 0.7 dynamic_slice.3
  12.4 0.7 broadcast_compare_fusion.1
  13.0 0.7 fusion.29
  13.7 50.4 %all-gather.2.cloned.1.call-done = bf16[768,4096]{1,0:T(8,128)(2,1)} async-done(((bf16[768,256]{1,0:T(8,128)(2,1)}), bf16[768,4096]{1,0:T(8,128)(2,1)}) %all-gather.2.cloned.1.call-update) | async-done | bytes 6291472 | tf_op jit(solution)/shard_map/all_gather | solution.py:64
  64.2 17.7 %fusion.23 = f32[768,2048]{1,0:T(8,128)S(1)} fusion(bf16[768,4096]{1,0:T(8,128)(2,1)} %all-gather.2.cloned.1.call-done, bf16[4096,2048]{1,0:T(8,128)(2,1)} %param.8), kind=kOutput, calls=%fused_computation.53 | convolution fusion | flops 12884901888 | bytes 29360128 | tf_op jit(solution)/shard_map/dot_general | solution.py:63
  81.9 0.0 copy-start
  81.9 0.6 select_reduce_fusion.1
  82.5 0.3 select_reduce_fusion.3
  82.9 0.9 select_reduce_fusion
  83.8 0.8 copy-done
  84.6 0.7 stack.2
  85.3 6.9 %all-to-all-start = ((f32[8,2,2048]{2,1,0:T(2,128)}), f32[8,2,2048]{2,1,0:T(2,128)S(1)}, u32[]{:S(2)}, u32[]{:S(2)}) async-start(f32[8,2,2048]{2,1,0:T(2,128)} %stack.2), calls=%async_computation | async-start | bytes 262144 | tf_op jit(solution)/shard_map/all_to_all | solution.py:79
  92.2 0.0 all-reduce.3.cloned.1.call-start
  92.2 2.1 select_reduce_fusion.2
  94.3 5.8 %all-to-all-done = f32[8,2,2048]{2,1,0:T(2,128)S(1)} async-done(((f32[8,2,2048]{2,1,0:T(2,128)}), f32[8,2,2048]{2,1,0:T(2,128)S(1)}, u32[]{:S(2)}, u32[]{:S(2)}) %all-to-all-start) | async-done | bytes 131104 | tf_op jit(solution)/shard_map/all_to_all | solution.py:79
  100.1 0.1 reshape.61
  100.2 0.2 fusion.12
  100.4 27.2 %psum.7 = f32[2,16]{1,0:T(2,128)S(1)} all-reduce(f32[2,16]{1,0:T(2,128)S(1)} %fusion.12), channel_id=1, replica_groups=mesh['dp'=8,'vocab'=16] {'vocab'}, use_global_device_ids=true, to_apply=%region_4.5 | all-reduce | flops 32 | bytes 256 | tf_op jit(solution)/shard_map/psum | solution.py:81
  127.6 0.1 fusion.18
  127.7 0.2 select_reduce_fusion.4
  127.9 0.5 fusion.22
  128.5 1.1 convolution_multiply_fusion
  129.6 0.0 all-reduce.3.cloned.1.call-update
  129.6 0.2 reduce-scatter.2.cloned.1.call-start
  129.8 0.3 fusion.6
  130.1 2.2 fusion.7
  132.3 77.5 %all-reduce.3.cloned.1.call-done = f32[16,2048]{1,0:T(8,128)} async-done(((f32[16,2048]{1,0:T(8,128)}), f32[16,2048]{1,0:T(8,128)}) %all-reduce.3.cloned.1.call-update) | async-done | bytes 131088
  209.7 0.9 fusion.10
  210.6 3.0 fusion
  213.6 19.4 %convolution_bitcast_fusion = f32[4096,768]{0,1:T(8,128)} fusion(bf16[4096,2048]{1,0:T(8,128)(2,1)} %param.8, bf16[512,2048]{1,0:T(8,128)(2,1)S(1)} %fusion, bf16[256,2048]{1,0:T(8,128)(2,1)S(1)} %fusion.7), kind=kOutput, calls=%fused_computation | convolution fusion | flops 12891193344 | bytes 32505856 | tf_op jit(solution)/shard_map/dot_general | solution.py:97
  233.0 0.0 reduce-scatter.2.cloned.1.call-update
  233.0 80.2 %reduce-scatter.2.cloned.1.call-done = f32[256,768]{0,1:T(8,128)} async-done(((f32[4096,768]{0,1:T(8,128)}), f32[256,768]{0,1:T(8,128)}) %reduce-scatter.2.cloned.1.call-update) | async-done | bytes 786448 | tf_op jit(solution)/shard_map/reduce_scatter | solution.py:96
  313.3 1.2 convert_bitcast_fusion
  314.4 0.7 slice.18
  315.1 0.7 slice.19
  (2 shorter events, 0.1 us)
Async XLA Ops:
  7.2 57.0 %all-gather.2.cloned.1.call-start = ((), (), s32[]{:S(2)}) async-start(), calls=%async_computation.2 | async-start | bytes 6684672 | tf_op jit(solution)/shard_map/all_gather | solution.py:64
  81.9 2.7 copy-start
  85.3 14.8 %all-to-all-start = ((f32[8,2,2048]{2,1,0:T(2,128)}), f32[8,2,2048]{2,1,0:T(2,128)S(1)}, u32[]{:S(2)}, u32[]{:S(2)}) async-start(f32[8,2,2048]{2,1,0:T(2,128)} %stack.2), calls=%async_computation | async-start | bytes 262144 | tf_op jit(solution)/shard_map/all_to_all | solution.py:79
  92.2 117.6 %all-reduce.3.cloned.1.call-start = ((), (), s32[]{:S(2)}) async-start(), calls=%async_computation.4 | async-start | bytes 262144
  129.6 183.7 %reduce-scatter.2.cloned.1.call-start = ((), (), s32[]{:S(2)}) async-start(), calls=%async_computation.3 | async-start | bytes 13369344 | tf_op jit(solution)/shard_map/reduce_scatter | solution.py:96
Sparse Core Ops, SparseCore 0:
  9.6 54.5 all-gather.1
  129.7 79.9 all-reduce.2
  233.2 80.0 reduce-scatter.1
